TPU v7x, 32 devices: a whole 2x2x4 slice. The times are simulated.
32 devices in a mesh: parts: 2 (over y), graph: 4 (over z), dp: 2 (over x), tensor: 2 (over core).
Axes of the slice: x: 2, y: 2, z: 4, core: 2. Of those that a mesh axis runs over, the one named last changes fastest.
Arguments:
- edges_in: bfloat16 [4, 4096, 512], P(('parts', 'dp'), 'graph', 'tensor'), parts along dimension 0, may hold values from -6 to 6
- weight: bfloat16 [512, 512], P(None, 'tensor'), may hold values from -0.25 to 0.25
- basis_tiles: bfloat16 [4, 144, 128, 128], P(('parts', 'dp'), 'graph'), parts along dimension 0, may hold values from -0.59765625 to 0.59765625
- target_blocks: int32 [4, 144], P(('parts', 'dp'), 'graph'), parts along dimension 0, may hold values from 0 to 7
- source_blocks: int32 [4, 144], P(('parts', 'dp'), 'graph'), parts along dimension 0, may hold values from 0 to 23
- counts: int32 [4, 4], P(('parts', 'dp'), 'graph'), parts along dimension 0, may hold values from 1 to 36, as said below
- grad_out: bfloat16 [4, 4096, 512], P(('parts', 'dp'), 'graph', 'tensor'), parts along dimension 0, may hold values from -6 to 6
Outputs:
- edges_out: bfloat16 [4, 4096, 512], P(('parts', 'dp'), 'graph', 'tensor'), parts along dimension 0
- grad_edges: bfloat16 [4, 4096, 512], P(('parts', 'dp'), 'graph', 'tensor'), parts along dimension 0
- grad_weight: float32 [1024, 512], P('parts', 'tensor'), parts along dimension 0
There are 2 independent parts, one for each index of `parts`. A program takes and returns all parts, laid end to end along the dimension named above; an argument that names none is the same for every part. Nothing has to cross between parts.
Inputs may be any that keep to these rules, and one draw needn't show every extreme that they name: `counts`: each shard has at least one live slot and some shard of every supercell has all 36 slots live; slots that are not live carry basis values that do not count.
All inputs are finite; a program needn't handle non-finite values.
Results may differ from a plain program's by a relative error of at most 0.0095.
Values may be sent and summed in bfloat16 or wider, within the bound.
No kernel may reach another device: no remote copies, remote signals or barrier semaphores. Data moves between devices by JAX's collectives and lax.ppermute only.
A program may use at most 64 MiB of HBM per device.

v0:
```python
import functools

import jax
import jax.numpy as jnp
from jax import lax
from jax.experimental import pallas as pl
from jax.experimental.pallas import tpu as pltpu
from jax.sharding import PartitionSpec as P

F32 = jnp.float32
BF16 = jnp.bfloat16
UNROLL = 4
LEAD = 4
FIRST = 4
BACK_COST, PREACT_COST, SLOPE_COST, SUM_COST, GATHER_COST, GRADS_COST = 1.0, 1.0, 0.5, 2.0, 3.0, 0.5
TICK_COSTS = (3.0, 0.3)
TRIPLET_COSTS = (0.5, 0.3, 0.3, 6.0)
VMEM = pl.BlockSpec(memory_space=pltpu.VMEM)
SMEM = pl.BlockSpec(memory_space=pltpu.SMEM)
HBM = pl.BlockSpec(memory_space=pltpu.HBM)
ANY = pl.BlockSpec(memory_space=pl.ANY)


def call(body, ins, outs, scratch=(), cost=0.0, space=None, limit=32, waits=(), carried=()):
    n, extra = len(ins), len(waits) + len(carried)

    def kernel(*refs):
        results = refs[n + extra :]
        body(*refs[:n], *results[: len(outs)], *results[len(outs) + len(carried) :])

    return pl.pallas_call(
        kernel,
        name=getattr(body, "func", body).__name__,
        in_specs=[space or (SMEM if x.dtype == jnp.int32 else VMEM) for x in ins] + [ANY] * extra,
        out_shape=[jax.ShapeDtypeStruct(s, d) for s, d in outs]
        + [jax.ShapeDtypeStruct(x.shape, x.dtype) for x in carried],
        out_specs=[VMEM for _ in outs] + [ANY for _ in carried],
        scratch_shapes=list(scratch),
        input_output_aliases={n + len(waits) + i: len(outs) + i for i in range(len(carried))},
        cost_estimate=pl.CostEstimate(flops=int(cost * 1.15e9), bytes_accessed=0, transcendentals=0),
        compiler_params=pltpu.CompilerParams(vmem_limit_bytes=limit * 1024 * 1024),
    )(*ins, *waits, *carried)


def shift(value, axis, steps):
    count = lax.axis_size(axis)
    return lax.ppermute(value, axis, [(i, (i + steps) % count) for i in range(count)])


def pick(listed, count, source, low, high):
    slots = source.shape[1]

    found = jnp.int32(0)
    for k in range(slots):
        listed[found] = k
        s = source[0, k]
        inside = (k < count) & (s >= low) & (s < high)
        found = found + inside.astype(jnp.int32)
    for j in range(UNROLL):
        listed[found + j] = 0
    return found


def over_tiles(listed, found, step):
    def some(i, carry):
        for j in range(UNROLL):
            at = i * UNROLL + j
            step(listed[at], at < found)
        return carry

    lax.fori_loop(0, (found + UNROLL - 1) // UNROLL, some, 0)


def back_body(ranges, nblocks, counts_hbm, target_hbm, source_hbm, tiles_hbm, grads_hbm, *rest):
    n = len(ranges)
    outs = rest[:n]
    acc, listed, counts, target, source, tiles, grads, sems = rest[n:]
    copies = [
        pltpu.make_async_copy(there, here, sems.at[i])
        for i, (there, here) in enumerate(
            [
                (counts_hbm, counts),
                (source_hbm, source),
                (target_hbm, target),
                (grads_hbm, grads),
                (tiles_hbm, tiles),
            ]
        )
    ]
    for copy in copies:
        copy.start()
    acc[...] = jnp.zeros_like(acc)
    for copy in copies[:3]:
        copy.wait()
    for low, out in zip(ranges, outs):
        if low != ranges[0]:
            acc[...] = jnp.zeros_like(acc)
        found = pick(listed, counts[0, 0], source, low, low + nblocks)
        if low == ranges[0]:
            for copy in copies[3:]:
                copy.wait()

        def step(k, valid):
            at = jnp.where(valid, source[0, k] - low, nblocks)
            acc[at] += lax.dot_general(
                tiles[k], grads[target[0, k]], (((0,), (0,)), ((), ())), preferred_element_type=F32
            )

        over_tiles(listed, found, step)
        for b in range(nblocks):
            out[b] = acc[b].astype(out.dtype)


def triplet_body(lows, nblocks, counts, target, source, tiles, *rest):
    n = len(lows)
    rows, start, out, acc, listed = rest[:n], *rest[n:]
    for b in range(nblocks):
        acc[b] = start[b].astype(F32)
    for low, piece in zip(lows, rows):
        found = pick(listed, counts[0, 0], source, low, low + piece.shape[0])

        def step(k, valid):
            at = jnp.where(valid, target[0, k], nblocks)
            s = jnp.where(valid, source[0, k] - low, 0)
            acc[at] += jnp.dot(tiles[k], piece[s], preferred_element_type=F32)

        over_tiles(listed, found, step)
    for b in range(nblocks):
        out[b] = acc[b].astype(out.dtype)


def preact_body(step, mine, theirs, weight, act, factor, flipped, up, *down):
    rows, chans = mine.shape
    core = lax.axis_index("tensor")
    own = pl.ds(pl.multiple_of(core * chans, chans), chans)
    other = pl.ds(pl.multiple_of((1 - core) * chans, chans), chans)
    for r in range(0, rows, step):
        at = pl.ds(r, step)
        pre = jnp.dot(mine[at], weight[own], preferred_element_type=F32) + jnp.dot(
            theirs[at], weight[other], preferred_element_type=F32
        )
        sig = 1.0 / (1.0 + jnp.exp(-pre))
        act[at] = (pre * sig).astype(BF16)
        factor[at] = sig * (1.0 + pre * (1.0 - sig))
        flipped[own, at] = mine[at].T
        flipped[other, at] = theirs[at].T
    up[...] = act[pl.ds(rows - up.shape[0], up.shape[0])]
    begin = 0
    for piece in down:
        piece[...] = act[pl.ds(begin, piece.shape[0])]
        begin += piece.shape[0]


def tick_body(out):
    out[...] = jnp.zeros_like(out)


def activate_body(mine, theirs, weight, act):
    chans = mine.shape[1]
    core = lax.axis_index("tensor")
    own = pl.ds(pl.multiple_of(core * chans, chans), chans)
    other = pl.ds(pl.multiple_of((1 - core) * chans, chans), chans)
    pre = jnp.dot(mine[...], weight[own], preferred_element_type=F32) + jnp.dot(
        theirs[...], weight[other], preferred_element_type=F32
    )
    act[...] = (pre / (1.0 + jnp.exp(-pre))).astype(BF16)


def partners():
    return [(f, d) for f in (0, 1) for d in range(lax.axis_size("dp")) if (f, d) != (0, 0)]


def to_partner(value, flip, steps):
    nz, ndp = lax.axis_size("graph"), lax.axis_size("dp")
    pairs = [
        (z * ndp + d, (z ^ flip) * ndp + (d + steps) % ndp) for z in range(nz) for d in range(ndp)
    ]
    return lax.ppermute(value, ("graph", "dp"), pairs)


def swap(value, bit):
    return lax.ppermute(value, "graph", [(z, z ^ bit) for z in range(lax.axis_size("graph"))])


def place(flip, steps, size):
    ndp = lax.axis_size("dp")
    d = lax.rem(lax.axis_index("dp") + steps + ndp, ndp)
    b = lax.rem(lax.axis_index("graph") + flip, 2)
    return pl.ds(pl.multiple_of((d * 2 + b) * size, size), size)


def slope_body(step, back, from_next, from_prev, factor, grads, weight, flipped, *rest):
    to_core, gsum, keep = rest[:3]
    others = partners()
    sends = rest[3 : 3 + len(others)]
    slope, part = rest[3 + len(others) :]
    rows, chans = grads.shape
    core = lax.axis_index("tensor")
    own = pl.ds(pl.multiple_of(core * chans, chans), chans)
    other = pl.ds(pl.multiple_of((1 - core) * chans, chans), chans)
    last = (((1,), (1,)), ((), ()))
    for r in range(0, rows, step):
        at = pl.ds(r, step)
        total = back[at] + from_next[at].astype(F32) + from_prev[at].astype(F32)
        piece = (total * factor[at]).astype(BF16)
        slope[at] = piece
        to_core[at] = lax.dot_general(piece, weight[other], last, preferred_element_type=F32).astype(BF16)
        gsum[at] = grads[at].astype(F32) + lax.dot_general(
            piece, weight[own], last, preferred_element_type=F32
        )
    part[...] = jnp.dot(flipped[...], slope[...], preferred_element_type=F32)
    size = keep.shape[0]
    keep[...] = part[place(0, 0, size)]
    for (flip, steps), send in zip(others, sends):
        send[...] = part[place(flip, steps, size)].astype(BF16)


def grads_body(gsum, arrived, out, token):
    token[...] = jnp.zeros_like(token)
    out[...] = (gsum[...] + arrived[...].astype(F32)).astype(BF16)


def total_body(scale, *refs):
    total = refs[0][...].astype(F32)
    for ref in refs[1:-1]:
        total = total + ref[...].astype(F32)
    refs[-1][...] = (total * scale).astype(BF16)


def gather_body(mine, *rest):
    out = rest[-1]
    size = mine.shape[0]
    out[place(0, 0, size)] = mine[...].astype(F32)
    for (flip, steps), ref in zip(partners(), rest):
        out[place(flip, -steps, size)] = ref[...].astype(F32)


def bits(nz):
    return [1 << i for i in range(1, nz.bit_length() - 1)]


def shards(edges_in, weight, basis_tiles, target_blocks, source_blocks, counts, grad_out):
    rows, chans = edges_in.shape[1], edges_in.shape[2]
    tile = basis_tiles.shape[2]
    nblocks = rows // tile
    slots = basis_tiles.shape[1]
    depth = weight.shape[0]
    ndp, nz = lax.axis_size("dp"), lax.axis_size("graph")
    mine, grads, tiles = edges_in[0], grad_out[0], basis_tiles[0]
    blocks = (nblocks, tile, chans)
    flat = (rows, chans)
    index = [counts, target_blocks, source_blocks, tiles]
    work = [pltpu.VMEM((nblocks + 1, tile, chans), F32), pltpu.SMEM((slots + UNROLL,), jnp.int32)]

    theirs = shift(mine, "tensor", 1)
    lead = min(LEAD, nblocks - 1)
    prev_rows = shift(mine[: lead * tile], "graph", 1)

    def back_terms(ranges, kinds, waits=()):
        return call(
            functools.partial(back_body, ranges, nblocks),
            [*index, grads.reshape(blocks)],
            [(blocks, kind) for kind in kinds],
            work
            + [pltpu.SMEM(x.shape, jnp.int32) for x in index[:3]]
            + [pltpu.VMEM(tiles.shape, BF16), pltpu.VMEM(blocks, BF16), pltpu.SemaphoreType.DMA((5,))],
            cost=BACK_COST,
            space=HBM,
            limit=58,
            waits=waits,
        )

    def tick(cost, *waits):
        return call(tick_body, [], [((8, 128), F32)], cost=cost, waits=waits)[0]

    def triplet(lows, pieces, start, kind, cost):
        return call(
            functools.partial(triplet_body, lows, nblocks),
            [*index, *pieces, start],
            [(blocks, kind)],
            work,
            cost=cost,
        )[0]

    (to_prev,) = back_terms((0,), (BF16,))
    from_next = shift(to_prev, "graph", -1)
    to_next, back = back_terms((2 * nblocks, nblocks), (BF16, F32), [to_prev])
    from_prev = shift(to_next, "graph", 1)
    cuts = [0, min(FIRST, nblocks - 1), nblocks]
    sizes = [nblocks - lead] + [high - low for low, high in zip(cuts, cuts[1:])]
    act, factor, flipped, *sent = call(
        functools.partial(preact_body, 256),
        [mine, theirs, weight],
        [(flat, BF16), (flat, F32), ((depth, rows), BF16)] + [((n * tile, chans), BF16) for n in sizes],
        cost=PREACT_COST,
    )
    up, first, second = [x.reshape(-1, tile, chans) for x in sent]
    prev_high = shift(up, "graph", 1)
    (prev_low,) = call(
        activate_body,
        [prev_rows, shift(prev_rows, "tensor", 1), weight],
        [((lead * tile, chans), BF16)],
        cost=PREACT_COST,
    )
    prev_low = prev_low.reshape(lead, tile, chans)
    others = partners()
    size = depth // (len(others) + 1)
    part = ((size, chans), BF16)
    to_core, gsum, keep, *sends, first = call(
        functools.partial(slope_body, 256),
        [back.reshape(flat), from_next.reshape(flat), from_prev.reshape(flat), factor, grads, weight, flipped],
        [(flat, BF16), (flat, F32), ((size, chans), F32)] + [part] * len(others),
        [pltpu.VMEM(flat, BF16), pltpu.VMEM((depth, chans), F32)],
        cost=SLOPE_COST,
        waits=[prev_low],
        carried=[first],
    )
    arrived = [to_partner(s, *at) for s, at in zip(sends, others)]
    next_first = shift(first, "graph", -1)
    summed = shift(to_core, "tensor", 1)
    grad_edges, token = call(grads_body, [gsum, summed], [(flat, BF16), ((8, 128), F32)], cost=GRADS_COST)
    acc = triplet((0, nblocks), (prev_low, act.reshape(blocks)), mine.reshape(blocks), F32, TRIPLET_COSTS[0])
    scale = float(1.0 / (ndp * edges_in.shape[0] * nz * rows) ** 0.5)
    stages = bits(nz)
    total, second = call(
        functools.partial(total_body, 1.0 if stages else scale),
        [keep, *arrived],
        [part],
        cost=SUM_COST,
        waits=[acc, tick(TICK_COSTS[0], prev_high)],
        carried=[second],
    )
    next_second = shift(second, "graph", -1)
    acc = triplet((lead,), (prev_high,), acc, F32, TRIPLET_COSTS[1])
    waits = [token, acc, tick(TICK_COSTS[1], next_first)]
    for bit in stages:
        (total,) = call(
            functools.partial(total_body, scale if bit == stages[-1] else 1.0),
            [total, swap(total, bit)],
            [part],
            cost=SUM_COST,
            waits=waits,
        )
    arrived = [to_partner(total, *at) for at in others]
    acc = triplet((2 * nblocks,), (next_first,), acc, F32, TRIPLET_COSTS[2])
    (grad_weight,) = call(
        gather_body,
        [total, *arrived],
        [((depth, chans), F32)],
        cost=GATHER_COST,
    )
    edges_out = triplet((2 * nblocks + cuts[1],), (next_second,), acc, BF16, TRIPLET_COSTS[3])
    return edges_out.reshape(1, rows, chans), grad_edges[None], grad_weight


def solution(mesh):
    placed = (
        P(("parts", "dp"), "graph", "tensor"),
        P(None, "tensor"),
        P(("parts", "dp"), "graph", None, None),
        P(("parts", "dp"), "graph"),
        P(("parts", "dp"), "graph"),
        P(("parts", "dp"), "graph"),
        P(("parts", "dp"), "graph", "tensor"),
    )
    return jax.shard_map(
        shards,
        mesh=mesh,
        in_specs=placed,
        out_specs=(
            P(("parts", "dp"), "graph", "tensor"),
            P(("parts", "dp"), "graph", "tensor"),
            P("parts", "tensor"),
        ),
        check_vma=False,
    )
```

profile of v0, /device:TPU:0, one launch (start us, length us, event | category | flops | bytes accessed | tf_op | source)
XLA Modules:
  0.0 64.2 jit_solution(8422180382561832935)
XLA Ops:
  1.1 1.0 %slice_bitcast_fusion = bf16[512,256]{1,0:T(8,128)(2,1)S(1)} fusion(bf16[1,1024,256]{2,1,0:T(8,128)(2,1)} %param.7), kind=kLoop, calls=%fused_computation | loop fusion | bytes 524288 | tf_op jit(solution)/shard_map/slice | solution.py:257
  2.1 2.6 %collective-permute-start.3 = (bf16[512,256]{1,0:T(8,128)(2,1)S(1)}, bf16[512,256]{1,0:T(8,128)(2,1)S(1)}, u32[]{:S(2)}, u32[]{:S(2)}) collective-permute-start(bf16[512,256]{1,0:T(8,128)(2,1)S(1)} %slice_bitcast_fusion), channel_id=1, source_target_pairs={{0,4},{4,8},{8,12},{12,0},{1,5},{5,9},{9,13},{13,1},{2,6},{6,10},{... | collective-permute-start | bytes 786440 | tf_op jit(solution)/shard_map/ppermute | solution.py:47
  5.4 2.6 %back_body.2.refs_5_ = bf16[8,128,256]{2,1,0:T(8,128)(2,1)} custom-call(s32[1,1]{1,0:T(1,128)S(6)} %copy.14.refs_0_, s32[1,36]{1,0:T(1,128)} %refs_1_.11, s32[1,36]{1,0:T(1,128)} %refs_2_.15, bf16[36,128,128]{2,1,0:T(8,128)(2,1)} %bitcast.17, bf16[8,128,256]{2,1,0:T(8,128)(2,1)} %bitcast.30), custom_call_target="tpu_custom_call" | custom-call | flops 1150000000 | tf_op jit(solution)/shard_map/back_body/pallas_call | solution.py:31
  8.0 2.4 %collective-permute-start = (bf16[8,128,256]{2,1,0:T(8,128)(2,1)}, bf16[8,128,256]{2,1,0:T(8,128)(2,1)S(1)}, u32[]{:S(2)}, u32[]{:S(2)}) collective-permute-start(bf16[8,128,256]{2,1,0:T(8,128)(2,1)} %back_body.2.refs_5_), channel_id=1, source_target_pairs={{0,12},{4,0},{8,4},{12,8},{1,13},{5,1},{9,5},{13,9},{2,14},{6,2},{... | collective-permute-start | bytes 1572872 | tf_op jit(solution)/shard_map/ppermute | solution.py:47
  10.4 3.6 %back_body.3 = (bf16[8,128,256]{2,1,0:T(8,128)(2,1)}, f32[8,128,256]{2,1,0:T(8,128)}) custom-call(s32[1,1]{1,0:T(1,128)S(6)} %copy.14.refs_0_, s32[1,36]{1,0:T(1,128)} %refs_1_.11, s32[1,36]{1,0:T(1,128)} %refs_2_.15, bf16[36,128,128]{2,1,0:T(8,128)(2,1)} %bitcast.18, bf16[8,128,256]{2,1,0:T(8,128)(2,1)} %bitcast.31, bf16[8,128,256]{2,1,0:T(8,128)(2,1)} %back_body.2.refs_5_), custom_call_target="tpu_custom_call" | custom-call | flops 1150000000 | tf_op jit(solution)/shard_map/back_body/pallas_call | solution.py:31
  15.1 2.3 %collective-permute-start.8 = (bf16[4,128,256]{2,1,0:T(8,128)(2,1)S(1)}, bf16[4,128,256]{2,1,0:T(8,128)(2,1)S(1)}, u32[]{:S(2)}, u32[]{:S(2)}) collective-permute-start(bf16[4,128,256]{2,1,0:T(8,128)(2,1)S(1)} %bitcast.37), channel_id=1, source_target_pairs={{0,4},{4,8},{8,12},{12,0},{1,5},{5,9},{9,13},{13,1},{2,6},{6,10},{... | collective-permute-start | bytes 786440 | tf_op jit(solution)/shard_map/ppermute | solution.py:47
  17.7 7.8 %collective-permute-done = bf16[8,128,256]{2,1,0:T(8,128)(2,1)S(1)} collective-permute-done((bf16[8,128,256]{2,1,0:T(8,128)(2,1)}, bf16[8,128,256]{2,1,0:T(8,128)(2,1)S(1)}, u32[]{:S(2)}, u32[]{:S(2)}) %collective-permute-start) | collective-permute-done | bytes 524320 | tf_op jit(solution)/shard_map/ppermute | solution.py:47
  25.5 11.6 %collective-permute-done.1 = bf16[8,128,256]{2,1,0:T(8,128)(2,1)S(1)} collective-permute-done((bf16[8,128,256]{2,1,0:T(8,128)(2,1)}, bf16[8,128,256]{2,1,0:T(8,128)(2,1)S(1)}, u32[]{:S(2)}, u32[]{:S(2)}) %collective-permute-start.1) | collective-permute-done | bytes 524320 | tf_op jit(solution)/shard_map/ppermute | solution.py:47
  37.1 0.9 %slope_body.1 = (bf16[1024,256]{1,0:T(8,128)(2,1)S(1)}, f32[1024,256]{1,0:T(8,128)S(1)}, f32[128,256]{1,0:T(8,128)S(1)}, bf16[128,256]{1,0:T(8,128)(2,1)S(1)}, b...) custom-call(f32[1024,256]{1,0:T(8,128)S(1)} %bitcast.26, ...), custom_call_target="tpu_custom_call", output_to_operand_aliasing={{6}: (8, {})} | custom-call | flops 575000000 | tf_op jit(solution)/shard_map/slope_body/pallas_call | solution.py:31
  38.0 1.0 %collective-permute-start.5 = (bf16[128,256]{1,0:T(8,128)(2,1)S(1)}, bf16[128,256]{1,0:T(8,128)(2,1)S(1)}, u32[]{:S(2)}, u32[]{:S(2)}) collective-permute-start(bf16[128,256]{1,0:T(8,128)(2,1)S(1)} %get-tuple-element.28), channel_id=1, source_target_pairs={{0,2},{2,0},{4,6},{6,4},{8,10},{10,8},{12,14},{14,12},{1,3},{3,1},... | collective-permute-start | bytes 196616 | tf_op jit(solution)/shard_map/ppermute | solution.py:178
  39.1 2.5 %collective-permute-start.7 = (bf16[128,256]{1,0:T(8,128)(2,1)S(1)}, bf16[128,256]{1,0:T(8,128)(2,1)S(1)}, u32[]{:S(2)}, u32[]{:S(2)}) collective-permute-start(bf16[128,256]{1,0:T(8,128)(2,1)S(1)} %get-tuple-element.30), channel_id=1, source_target_pairs={{0,6},{2,4},{4,2},{6,0},{8,14},{10,12},{12,10},{14,8},{1,7},{3,5},... | collective-permute-start | bytes 196616 | tf_op jit(solution)/shard_map/ppermute | solution.py:178
  41.6 0.9 %collective-permute-start.10 = (bf16[4,128,256]{2,1,0:T(8,128)(2,1)S(1)}, bf16[4,128,256]{2,1,0:T(8,128)(2,1)S(1)}, u32[]{:S(2)}, u32[]{:S(2)}) collective-permute-start(bf16[4,128,256]{2,1,0:T(8,128)(2,1)S(1)} %get-tuple-element.35), channel_id=1, source_target_pairs={{0,12},{4,0},{8,4},{12,8},{1,13},{5,1},{9,5},{13,9},{2,14},{6,2},{... | collective-permute-start | bytes 786440 | tf_op jit(solution)/shard_map/ppermute | solution.py:47
  42.5 1.3 %triplet_body.4.refs_4_.refs_5_ = f32[8,128,256]{2,1,0:T(8,128)S(1)} custom-call(s32[1,1]{1,0:T(1,128)S(6)} %copy.14.refs_0_, s32[1,36]{1,0:T(1,128)S(1)} %copy-done.5, s32[1,36]{1,0:T(1,128)S(1)} %copy-done.6, bf16[36,128,128]{2,1,0:T(8,128)(2,1)S(1)} %bitcast.19, bf16[4,128,256]{2,1,0:T(8,128)(2,1)S(1)} %bitcast.28, bf16[8,128,256]{2,1,0:T(8,128)(2,1)S(1)} %bitcast.29, ...), custom_call_target="tpu_custom_call" | custom-call | flops 575000000 | tf_op jit(solution)/shard_map/triplet_body/pallas_call | solution.py:31
  44.1 1.9 %collective-permute-done.7.refs_3_ = bf16[128,256]{1,0:T(8,128)(2,1)S(1)} collective-permute-done((bf16[128,256]{1,0:T(8,128)(2,1)S(1)}, bf16[128,256]{1,0:T(8,128)(2,1)S(1)}, u32[]{:S(2)}, u32[]{:S(2)}) %collective-permute-start.7) | collective-permute-done | bytes 65568 | tf_op jit(solution)/shard_map/ppermute | solution.py:178
  46.0 1.0 %collective-permute-start.12 = (bf16[128,256]{1,0:T(8,128)(2,1)S(1)}, bf16[128,256]{1,0:T(8,128)(2,1)S(1)}, u32[]{:S(2)}, u32[]{:S(2)}) collective-permute-start(bf16[128,256]{1,0:T(8,128)(2,1)S(1)} %get-tuple-element.39.refs_0_), channel_id=1, source_target_pairs={{0,8},{4,12},{8,0},{12,4},{1,9},{5,13},{9,1},{13,5},{2,10},{6,14},... | collective-permute-start | bytes 196616 | tf_op jit(solution)/shard_map/ppermute | solution.py:182
  47.0 2.3 %collective-permute-start.9 = (bf16[4,128,256]{2,1,0:T(8,128)(2,1)S(1)}, bf16[4,128,256]{2,1,0:T(8,128)(2,1)S(1)}, u32[]{:S(2)}, u32[]{:S(2)}) collective-permute-start(bf16[4,128,256]{2,1,0:T(8,128)(2,1)S(1)} %get-tuple-element.34), channel_id=1, source_target_pairs={{0,12},{4,0},{8,4},{12,8},{1,13},{5,1},{9,5},{13,9},{2,14},{6,2},{... | collective-permute-start | bytes 786440 | tf_op jit(solution)/shard_map/ppermute | solution.py:47
  49.4 1.0 %triplet_body.5.refs_5_.refs_3_ = f32[8,128,256]{2,1,0:T(8,128)S(1)} custom-call(s32[1,1]{1,0:T(1,128)S(6)} %copy.14.refs_0_, s32[1,36]{1,0:T(1,128)S(1)} %copy-done.5, s32[1,36]{1,0:T(1,128)S(1)} %copy-done.6, bf16[36,128,128]{2,1,0:T(8,128)(2,1)S(1)} %bitcast.20, bf16[4,128,256]{2,1,0:T(8,128)(2,1)S(1)} %collective-permute-done.8.refs_0_.refs_4_, ...), custom_call_target="tpu_custom_call" | custom-call | flops 345000000 | tf_op jit(solution)/shard_map/triplet_body/pallas_call | solution.py:31
  50.4 1.9 %collective-permute-done.10.refs_4_.refs_0_ = bf16[4,128,256]{2,1,0:T(8,128)(2,1)S(1)} collective-permute-done((bf16[4,128,256]{2,1,0:T(8,128)(2,1)S(1)}, bf16[4,128,256]{2,1,0:T(8,128)(2,1)S(1)}, u32[]{:S(2)}, u32[]{:S(2)}) %collective-permute-start.10) | collective-permute-done | bytes 262176 | tf_op jit(solution)/shard_map/ppermute | solution.py:47
  52.2 1.0 %triplet_body.6.refs_5_ = f32[8,128,256]{2,1,0:T(8,128)S(1)} custom-call(s32[1,1]{1,0:T(1,128)S(6)} %copy.14.refs_0_, s32[1,36]{1,0:T(1,128)S(1)} %copy-done.5, s32[1,36]{1,0:T(1,128)S(1)} %copy-done.6, bf16[36,128,128]{2,1,0:T(8,128)(2,1)S(1)} %bitcast.21, bf16[4,128,256]{2,1,0:T(8,128)(2,1)S(1)} %collective-permute-done.10.refs_4_.refs_0_, ...), custom_call_target="tpu_custom_call" | custom-call | flops 345000000 | tf_op jit(solution)/shard_map/triplet_body/pallas_call | solution.py:31
  53.2 0.9 %grads_body.1 = (bf16[1024,256]{1,0:T(8,128)(2,1)}, f32[8,128]{1,0:T(8,128)S(1)}) custom-call(f32[1024,256]{1,0:T(8,128)S(1)} %get-tuple-element.36.refs_0_, bf16[1024,256]{1,0:T(8,128)(2,1)S(1)} %collective-permute-done.11.refs_1_), custom_call_target="tpu_custom_call" | custom-call | flops 575000000 | tf_op jit(solution)/shard_map/grads_body/pallas_call | solution.py:31
  54.1 4.9 %collective-permute-start.15 = (bf16[128,256]{1,0:T(8,128)(2,1)S(1)}, bf16[128,256]{1,0:T(8,128)(2,1)S(1)}, u32[]{:S(2)}, u32[]{:S(2)}) collective-permute-start(bf16[128,256]{1,0:T(8,128)(2,1)S(1)} %total_body.3.refs_0_), channel_id=1, source_target_pairs={{0,6},{2,4},{4,2},{6,0},{8,14},{10,12},{12,10},{14,8},{1,7},{3,5},... | collective-permute-start | bytes 196616 | tf_op jit(solution)/shard_map/ppermute | solution.py:178
  59.7 1.8 %triplet_body.7 = bf16[8,128,256]{2,1,0:T(8,128)(2,1)} custom-call(s32[1,1]{1,0:T(1,128)S(6)} %copy.14.refs_0_, s32[1,36]{1,0:T(1,128)S(1)} %copy-done.5, s32[1,36]{1,0:T(1,128)S(1)} %copy-done.6, bf16[36,128,128]{2,1,0:T(8,128)(2,1)S(1)} %bitcast.22, bf16[4,128,256]{2,1,0:T(8,128)(2,1)S(1)} %collective-permute-done.9.refs_4_, ...), custom_call_target="tpu_custom_call" | custom-call | flops 6899999744 | tf_op jit(solution)/shard_map/triplet_body/pallas_call | solution.py:31
  61.5 1.9 %collective-permute-done.14.refs_2_ = bf16[128,256]{1,0:T(8,128)(2,1)S(1)} collective-permute-done((bf16[128,256]{1,0:T(8,128)(2,1)S(1)}, bf16[128,256]{1,0:T(8,128)(2,1)S(1)}, u32[]{:S(2)}, u32[]{:S(2)}) %collective-permute-start.14) | collective-permute-done | bytes 65568 | tf_op jit(solution)/shard_map/ppermute | solution.py:178
  63.3 0.8 %gather_body.1 = f32[512,256]{1,0:T(8,128)} custom-call(bf16[128,256]{1,0:T(8,128)(2,1)S(1)} %total_body.3.refs_0_, bf16[128,256]{1,0:T(8,128)(2,1)S(1)} %collective-permute-done.13.refs_1_, bf16[128,256]{1,0:T(8,128)(2,1)S(1)} %collective-permute-done.14.refs_2_, bf16[128,256]{1,0:T(8,128)(2,1)S(1)} %collective-permute-done.15.refs_3_), custom_call_target="tpu_custom_call" | custom-call | flops 3449999872 | tf_op jit(solution)/shard_map/gather_body/pallas_call | solution.py:31
  (38 shorter events, 2.8 us)
Async XLA Ops:
  0.6 13.7 %collective-permute-start.2 = (bf16[1024,256]{1,0:T(8,128)(2,1)}, bf16[1024,256]{1,0:T(8,128)(2,1)S(1)}, u32[]{:S(2)}, u32[]{:S(2)}) collective-permute-start(bf16[1024,256]{1,0:T(8,128)(2,1)} %bitcast.23), channel_id=1, source_target_pairs={{0,1},{1,0},{2,3},{3,2},{4,5},{5,4},{6,7},{7,6},{8,9},{9,8},{10,11... | collective-permute-start | bytes 1572872 | tf_op jit(solution)/shard_map/ppermute | solution.py:47
  2.1 11.9 %collective-permute-start.3 = (bf16[512,256]{1,0:T(8,128)(2,1)S(1)}, bf16[512,256]{1,0:T(8,128)(2,1)S(1)}, u32[]{:S(2)}, u32[]{:S(2)}) collective-permute-start(bf16[512,256]{1,0:T(8,128)(2,1)S(1)} %slice_bitcast_fusion), channel_id=1, source_target_pairs={{0,4},{4,8},{8,12},{12,0},{1,5},{5,9},{9,13},{13,1},{2,6},{6,10},{... | collective-permute-start | bytes 786440 | tf_op jit(solution)/shard_map/ppermute | solution.py:47
  8.0 6.3 %copy-start.1 = (bf16[1,1024,256]{2,1,0:T(8,128)(2,1)S(1)}, bf16[1,1024,256]{2,1,0:T(8,128)(2,1)}, u32[]{:S(2)}) copy-start(bf16[1,1024,256]{2,1,0:T(8,128)(2,1)} %param.7) | copy-start | bytes 1572868
  8.0 6.3 %copy-start.4 = (bf16[512,256]{1,0:T(8,128)(2,1)S(1)}, bf16[512,256]{1,0:T(8,128)(2,1)}, u32[]{:S(2)}) copy-start(bf16[512,256]{1,0:T(8,128)(2,1)} %refs_5_.1) | copy-start | bytes 786436
  8.0 17.5 %collective-permute-start = (bf16[8,128,256]{2,1,0:T(8,128)(2,1)}, bf16[8,128,256]{2,1,0:T(8,128)(2,1)S(1)}, u32[]{:S(2)}, u32[]{:S(2)}) collective-permute-start(bf16[8,128,256]{2,1,0:T(8,128)(2,1)} %back_body.2.refs_5_), channel_id=1, source_target_pairs={{0,12},{4,0},{8,4},{12,8},{1,13},{5,1},{9,5},{13,9},{2,14},{6,2},{... | collective-permute-start | bytes 1572872 | tf_op jit(solution)/shard_map/ppermute | solution.py:47
  14.0 23.1 %collective-permute-start.1 = (bf16[8,128,256]{2,1,0:T(8,128)(2,1)}, bf16[8,128,256]{2,1,0:T(8,128)(2,1)S(1)}, u32[]{:S(2)}, u32[]{:S(2)}) collective-permute-start(bf16[8,128,256]{2,1,0:T(8,128)(2,1)} %get-tuple-element.23), channel_id=1, source_target_pairs={{0,4},{4,8},{8,12},{12,0},{1,5},{5,9},{9,13},{13,1},{2,6},{6,10},{... | collective-permute-start | bytes 1572872 | tf_op jit(solution)/shard_map/ppermute | solution.py:47
  14.1 3.3 %collective-permute-start.4 = (bf16[512,256]{1,0:T(8,128)(2,1)S(1)}, bf16[512,256]{1,0:T(8,128)(2,1)S(1)}, u32[]{:S(2)}, u32[]{:S(2)}) collective-permute-start(bf16[512,256]{1,0:T(8,128)(2,1)S(1)} %collective-permute-done.3.refs_0_), channel_id=1, source_target_pairs={{0,1},{1,0},{2,3},{3,2},{4,5},{5,4},{6,7},{7,6},{8,9},{9,8},{10,11... | collective-permute-start | bytes 786440 | tf_op jit(solution)/shard_map/ppermute | solution.py:47
  15.1 22.0 %copy-start.2 = (f32[8,128,256]{2,1,0:T(8,128)S(1)}, f32[8,128,256]{2,1,0:T(8,128)}, u32[]{:S(2)}) copy-start(f32[8,128,256]{2,1,0:T(8,128)} %get-tuple-element.22) | copy-start | bytes 3145732
  15.1 22.0 %copy-start.3 = (bf16[1,1024,256]{2,1,0:T(8,128)(2,1)S(1)}, bf16[1,1024,256]{2,1,0:T(8,128)(2,1)}, u32[]{:S(2)}) copy-start(bf16[1,1024,256]{2,1,0:T(8,128)(2,1)} %param.13) | copy-start | bytes 1572868
  15.1 28.8 %collective-permute-start.8 = (bf16[4,128,256]{2,1,0:T(8,128)(2,1)S(1)}, bf16[4,128,256]{2,1,0:T(8,128)(2,1)S(1)}, u32[]{:S(2)}, u32[]{:S(2)}) collective-permute-start(bf16[4,128,256]{2,1,0:T(8,128)(2,1)S(1)} %bitcast.37), channel_id=1, source_target_pairs={{0,4},{4,8},{8,12},{12,0},{1,5},{5,9},{9,13},{13,1},{2,6},{6,10},{... | collective-permute-start | bytes 786440 | tf_op jit(solution)/shard_map/ppermute | solution.py:47
  37.1 5.4 %copy-start = (bf16[1,36,128,128]{3,2,1,0:T(8,128)(2,1)S(1)}, bf16[1,36,128,128]{3,2,1,0:T(8,128)(2,1)}, u32[]{:S(2)}) copy-start(bf16[1,36,128,128]{3,2,1,0:T(8,128)(2,1)} %param.9) | copy-start | bytes 3538948
  37.1 5.4 %copy-start.5 = (s32[1,36]{1,0:T(1,128)S(1)}, s32[1,36]{1,0:T(1,128)}, u32[]{:S(2)}) copy-start(s32[1,36]{1,0:T(1,128)} %refs_1_.11) | copy-start | bytes 436
  37.1 5.4 %copy-start.6 = (s32[1,36]{1,0:T(1,128)S(1)}, s32[1,36]{1,0:T(1,128)}, u32[]{:S(2)}) copy-start(s32[1,36]{1,0:T(1,128)} %refs_2_.15) | copy-start | bytes 436
  38.0 6.0 %collective-permute-start.5 = (bf16[128,256]{1,0:T(8,128)(2,1)S(1)}, bf16[128,256]{1,0:T(8,128)(2,1)S(1)}, u32[]{:S(2)}, u32[]{:S(2)}) collective-permute-start(bf16[128,256]{1,0:T(8,128)(2,1)S(1)} %get-tuple-element.28), channel_id=1, source_target_pairs={{0,2},{2,0},{4,6},{6,4},{8,10},{10,8},{12,14},{14,12},{1,3},{3,1},... | collective-permute-start | bytes 196616 | tf_op jit(solution)/shard_map/ppermute | solution.py:178
  39.0 5.1 %collective-permute-start.6 = (bf16[128,256]{1,0:T(8,128)(2,1)S(1)}, bf16[128,256]{1,0:T(8,128)(2,1)S(1)}, u32[]{:S(2)}, u32[]{:S(2)}) collective-permute-start(bf16[128,256]{1,0:T(8,128)(2,1)S(1)} %get-tuple-element.29), channel_id=1, source_target_pairs={{0,4},{2,6},{4,0},{6,2},{8,12},{10,14},{12,8},{14,10},{1,5},{3,7},... | collective-permute-start | bytes 196616 | tf_op jit(solution)/shard_map/ppermute | solution.py:178
  39.1 6.9 %collective-permute-start.7 = (bf16[128,256]{1,0:T(8,128)(2,1)S(1)}, bf16[128,256]{1,0:T(8,128)(2,1)S(1)}, u32[]{:S(2)}, u32[]{:S(2)}) collective-permute-start(bf16[128,256]{1,0:T(8,128)(2,1)S(1)} %get-tuple-element.30), channel_id=1, source_target_pairs={{0,6},{2,4},{4,2},{6,0},{8,14},{10,12},{12,10},{14,8},{1,7},{3,5},... | collective-permute-start | bytes 196616 | tf_op jit(solution)/shard_map/ppermute | solution.py:178
  41.6 10.6 %collective-permute-start.10 = (bf16[4,128,256]{2,1,0:T(8,128)(2,1)S(1)}, bf16[4,128,256]{2,1,0:T(8,128)(2,1)S(1)}, u32[]{:S(2)}, u32[]{:S(2)}) collective-permute-start(bf16[4,128,256]{2,1,0:T(8,128)(2,1)S(1)} %get-tuple-element.35), channel_id=1, source_target_pairs={{0,12},{4,0},{8,4},{12,8},{1,13},{5,1},{9,5},{13,9},{2,14},{6,2},{... | collective-permute-start | bytes 786440 | tf_op jit(solution)/shard_map/ppermute | solution.py:47
  43.9 9.3 %collective-permute-start.11 = (bf16[1024,256]{1,0:T(8,128)(2,1)S(1)}, bf16[1024,256]{1,0:T(8,128)(2,1)S(1)}, u32[]{:S(2)}, u32[]{:S(2)}) collective-permute-start(bf16[1024,256]{1,0:T(8,128)(2,1)S(1)} %get-tuple-element.37), channel_id=1, source_target_pairs={{0,1},{1,0},{2,3},{3,2},{4,5},{5,4},{6,7},{7,6},{8,9},{9,8},{10,11... | collective-permute-start | bytes 1572872 | tf_op jit(solution)/shard_map/ppermute | solution.py:47
  46.0 8.1 %collective-permute-start.12 = (bf16[128,256]{1,0:T(8,128)(2,1)S(1)}, bf16[128,256]{1,0:T(8,128)(2,1)S(1)}, u32[]{:S(2)}, u32[]{:S(2)}) collective-permute-start(bf16[128,256]{1,0:T(8,128)(2,1)S(1)} %get-tuple-element.39.refs_0_), channel_id=1, source_target_pairs={{0,8},{4,12},{8,0},{12,4},{1,9},{5,13},{9,1},{13,5},{2,10},{6,14},... | collective-permute-start | bytes 196616 | tf_op jit(solution)/shard_map/ppermute | solution.py:182
  47.0 12.7 %collective-permute-start.9 = (bf16[4,128,256]{2,1,0:T(8,128)(2,1)S(1)}, bf16[4,128,256]{2,1,0:T(8,128)(2,1)S(1)}, u32[]{:S(2)}, u32[]{:S(2)}) collective-permute-start(bf16[4,128,256]{2,1,0:T(8,128)(2,1)S(1)} %get-tuple-element.34), channel_id=1, source_target_pairs={{0,12},{4,0},{8,4},{12,8},{1,13},{5,1},{9,5},{13,9},{2,14},{6,2},{... | collective-permute-start | bytes 786440 | tf_op jit(solution)/shard_map/ppermute | solution.py:47
  54.1 7.3 %collective-permute-start.15 = (bf16[128,256]{1,0:T(8,128)(2,1)S(1)}, bf16[128,256]{1,0:T(8,128)(2,1)S(1)}, u32[]{:S(2)}, u32[]{:S(2)}) collective-permute-start(bf16[128,256]{1,0:T(8,128)(2,1)S(1)} %total_body.3.refs_0_), channel_id=1, source_target_pairs={{0,6},{2,4},{4,2},{6,0},{8,14},{10,12},{12,10},{14,8},{1,7},{3,5},... | collective-permute-start | bytes 196616 | tf_op jit(solution)/shard_map/ppermute | solution.py:178
  59.0 4.3 %collective-permute-start.14 = (bf16[128,256]{1,0:T(8,128)(2,1)S(1)}, bf16[128,256]{1,0:T(8,128)(2,1)S(1)}, u32[]{:S(2)}, u32[]{:S(2)}) collective-permute-start(bf16[128,256]{1,0:T(8,128)(2,1)S(1)} %total_body.3.refs_0_), channel_id=1, source_target_pairs={{0,4},{2,6},{4,0},{6,2},{8,12},{10,14},{12,8},{14,10},{1,5},{3,7},... | collective-permute-start | bytes 196616 | tf_op jit(solution)/shard_map/ppermute | solution.py:178
  59.0 4.3 %collective-permute-start.13 = (bf16[128,256]{1,0:T(8,128)(2,1)S(1)}, bf16[128,256]{1,0:T(8,128)(2,1)S(1)}, u32[]{:S(2)}, u32[]{:S(2)}) collective-permute-start(bf16[128,256]{1,0:T(8,128)(2,1)S(1)} %total_body.3.refs_0_), channel_id=1, source_target_pairs={{0,2},{2,0},{4,6},{6,4},{8,10},{10,8},{12,14},{14,12},{1,3},{3,1},... | collective-permute-start | bytes 196616 | tf_op jit(solution)/shard_map/ppermute | solution.py:178
where the time goes:
time: 64.5 us; the launch traced here: 64.2 us
  waiting for transfers between devices  25.2 us (39%)
  starting transfers between devices  21.6 us (33%)
  Pallas kernels  14.9 us (23%)
  between operations  1.47 us (2%)
  local copies, waits for them, and re-layouts  1 us (2%)
    ppermute x9, waiting for transfers between devices, shift(): lax.ppermute(value, axis, [(i, (i + steps) % count) for i in range(count)])  21.3 us
    pallas_call x15, Pallas kernels, call(): pl.pallas_call(kernel, name=getattr(body, 'func', body).__name__, in_spec...  14.9 us
    ppermute x9, starting transfers between devices, shift(): lax.ppermute(value, axis, [(i, (i + steps) % count) for i in range(count)])  11.5 us
    ppermute x6, starting transfers between devices, to_partner(): return lax.ppermute(value, ('graph', 'dp'), pairs)  9.1 us
    ppermute x6, waiting for transfers between devices, to_partner(): return lax.ppermute(value, ('graph', 'dp'), pairs)  3.86 us
  transfers between devices with their start and end apart: 16, of which 6 were waited for; matrix products, arithmetic and copies ran while one was open for 2% of the time, Pallas kernels for 22%

commit v1 on v0

--- a/solution.py
+++ b/solution.py
@@ -11,7 +11,7 @@
 BF16 = jnp.bfloat16
 UNROLL = 4
 LEAD = 4
-FIRST = 4
+FIRST = 5
 BACK_COST, PREACT_COST, SLOPE_COST, SUM_COST, GATHER_COST, GRADS_COST = 1.0, 1.0, 0.5, 2.0, 3.0, 0.5
 TICK_COSTS = (3.0, 0.3)
 TRIPLET_COSTS = (0.5, 0.3, 0.3, 6.0)

time: 64.5 us -> 64.6 us (level)
  starting transfers between devices: 21.6 us -> 18.3 us
  Pallas kernels: 14.9 us -> 17.7 us
  waiting for transfers between devices: 25.2 us -> 25.9 us
    pallas_call x15, Pallas kernels: 14.9 us -> 17.7 us  [call(): pl.pallas_call(kernel, name=getattr(body, 'func', body).__name__, in_spec...]
    ppermute x9, starting transfers between devices: 11.5 us -> 9.36 us  [shift(): lax.ppermute(value, axis, [(i, (i + steps) % count) for i in range(count)])]
    ppermute x6, starting transfers between devices: 9.1 us -> 7.24 us  [to_partner(): return lax.ppermute(value, ('graph', 'dp'), pairs)]
    ppermute x9, waiting for transfers between devices: 21.3 us -> 23 us  [shift(): lax.ppermute(value, axis, [(i, (i + steps) % count) for i in range(count)])]
    ppermute x6, waiting for transfers between devices: 3.86 us -> 2.92 us  [to_partner(): return lax.ppermute(value, ('graph', 'dp'), pairs)]
    ppermute x1, starting transfers between devices: 1 us -> 1.69 us  [swap(): lax.ppermute(value, 'graph', [(z, z ^ bit) for z in range(lax.axis_size('...]
  transfers between devices with their start and end apart: 16 -> 16, of which waited for: 6 -> 6; matrix products, arithmetic and copies ran while one was open for 2% -> 2% of each run, Pallas kernels for 22% -> 26%
where the time goes in v1:
time: 64.6 us; the launch traced here: 64.3 us
  waiting for transfers between devices  25.9 us (40%)
  starting transfers between devices  18.3 us (28%)
  Pallas kernels  17.7 us (27%)
  between operations  1.48 us (2%)
  local copies, waits for them, and re-layouts  1 us (2%)
    ppermute x9, waiting for transfers between devices, shift(): lax.ppermute(value, axis, [(i, (i + steps) % count) for i in range(count)])  23 us
    pallas_call x15, Pallas kernels, call(): pl.pallas_call(kernel, name=getattr(body, 'func', body).__name__, in_spec...  17.7 us
    ppermute x9, starting transfers between devices, shift(): lax.ppermute(value, axis, [(i, (i + steps) % count) for i in range(count)])  9.36 us
    ppermute x6, starting transfers between devices, to_partner(): return lax.ppermute(value, ('graph', 'dp'), pairs)  7.24 us
    ppermute x6, waiting for transfers between devices, to_partner(): return lax.ppermute(value, ('graph', 'dp'), pairs)  2.92 us
    ppermute x1, starting transfers between devices, swap(): lax.ppermute(value, 'graph', [(z, z ^ bit) for z in range(lax.axis_size('...  1.69 us
  transfers between devices with their start and end apart: 16, of which 6 were waited for; matrix products, arithmetic and copies ran while one was open for 2% of the time, Pallas kernels for 26%

profile of v1, /device:TPU:0, one launch (start us, length us, event | category | flops | bytes accessed | tf_op | source)
XLA Modules:
  0.0 64.3 jit_solution(417083559856709035)
XLA Ops:
  1.1 1.0 %slice_bitcast_fusion = bf16[512,256]{1,0:T(8,128)(2,1)S(1)} fusion(bf16[1,1024,256]{2,1,0:T(8,128)(2,1)} %param.7), kind=kLoop, calls=%fused_computation | loop fusion | bytes 524288 | tf_op jit(solution)/shard_map/slice | solution.py:257
  2.1 2.6 %collective-permute-start.3 = (bf16[512,256]{1,0:T(8,128)(2,1)S(1)}, bf16[512,256]{1,0:T(8,128)(2,1)S(1)}, u32[]{:S(2)}, u32[]{:S(2)}) collective-permute-start(bf16[512,256]{1,0:T(8,128)(2,1)S(1)} %slice_bitcast_fusion), channel_id=1, source_target_pairs={{0,4},{4,8},{8,12},{12,0},{1,5},{5,9},{9,13},{13,1},{2,6},{6,10},{... | collective-permute-start | bytes 786440 | tf_op jit(solution)/shard_map/ppermute | solution.py:47
  5.4 3.1 %back_body.2.refs_5_ = bf16[8,128,256]{2,1,0:T(8,128)(2,1)} custom-call(s32[1,1]{1,0:T(1,128)S(6)} %copy.14.refs_0_, s32[1,36]{1,0:T(1,128)} %refs_1_.11, s32[1,36]{1,0:T(1,128)} %refs_2_.15, bf16[36,128,128]{2,1,0:T(8,128)(2,1)} %bitcast.17, bf16[8,128,256]{2,1,0:T(8,128)(2,1)} %bitcast.30), custom_call_target="tpu_custom_call" | custom-call | flops 1150000000 | tf_op jit(solution)/shard_map/back_body/pallas_call | solution.py:31
  8.6 1.6 %collective-permute-start = (bf16[8,128,256]{2,1,0:T(8,128)(2,1)}, bf16[8,128,256]{2,1,0:T(8,128)(2,1)S(1)}, u32[]{:S(2)}, u32[]{:S(2)}) collective-permute-start(bf16[8,128,256]{2,1,0:T(8,128)(2,1)} %back_body.2.refs_5_), channel_id=1, source_target_pairs={{0,12},{4,0},{8,4},{12,8},{1,13},{5,1},{9,5},{13,9},{2,14},{6,2},{... | collective-permute-start | bytes 1572872 | tf_op jit(solution)/shard_map/ppermute | solution.py:47
  10.1 4.7 %back_body.3 = (bf16[8,128,256]{2,1,0:T(8,128)(2,1)}, f32[8,128,256]{2,1,0:T(8,128)}) custom-call(s32[1,1]{1,0:T(1,128)S(6)} %copy.14.refs_0_, s32[1,36]{1,0:T(1,128)} %refs_1_.11, s32[1,36]{1,0:T(1,128)} %refs_2_.15, bf16[36,128,128]{2,1,0:T(8,128)(2,1)} %bitcast.18, bf16[8,128,256]{2,1,0:T(8,128)(2,1)} %bitcast.31, bf16[8,128,256]{2,1,0:T(8,128)(2,1)} %back_body.2.refs_5_), custom_call_target="tpu_custom_call" | custom-call | flops 1150000000 | tf_op jit(solution)/shard_map/back_body/pallas_call | solution.py:31
  15.2 0.7 %preact_body.1 = (bf16[1024,256]{1,0:T(8,128)(2,1)S(1)}, f32[1024,256]{1,0:T(8,128)S(1)}, bf16[512,1024]{1,0:T(8,128)(2,1)S(1)}, bf16[512,256]{1,0:T(8,128)(2,1)...) custom-call(bf16[1024,256]{1,0:T(8,128)(2,1)S(1)} %bitcast.24, ...), custom_call_target="tpu_custom_call" | custom-call | flops 1150000000 | tf_op jit(solution)/shard_map/preact_body/pallas_call | solution.py:31
  16.8 8.4 %collective-permute-done = bf16[8,128,256]{2,1,0:T(8,128)(2,1)S(1)} collective-permute-done((bf16[8,128,256]{2,1,0:T(8,128)(2,1)}, bf16[8,128,256]{2,1,0:T(8,128)(2,1)S(1)}, u32[]{:S(2)}, u32[]{:S(2)}) %collective-permute-start) | collective-permute-done | bytes 524320 | tf_op jit(solution)/shard_map/ppermute | solution.py:47
  25.2 11.2 %collective-permute-done.1 = bf16[8,128,256]{2,1,0:T(8,128)(2,1)S(1)} collective-permute-done((bf16[8,128,256]{2,1,0:T(8,128)(2,1)}, bf16[8,128,256]{2,1,0:T(8,128)(2,1)S(1)}, u32[]{:S(2)}, u32[]{:S(2)}) %collective-permute-start.1) | collective-permute-done | bytes 524320 | tf_op jit(solution)/shard_map/ppermute | solution.py:47
  36.4 0.9 %slope_body.1 = (bf16[1024,256]{1,0:T(8,128)(2,1)S(1)}, f32[1024,256]{1,0:T(8,128)S(1)}, f32[128,256]{1,0:T(8,128)S(1)}, bf16[128,256]{1,0:T(8,128)(2,1)S(1)}, b...) custom-call(f32[1024,256]{1,0:T(8,128)S(1)} %bitcast.26, ...), custom_call_target="tpu_custom_call", output_to_operand_aliasing={{6}: (8, {})} | custom-call | flops 575000000 | tf_op jit(solution)/shard_map/slope_body/pallas_call | solution.py:31
  37.3 1.8 %collective-permute-start.5 = (bf16[128,256]{1,0:T(8,128)(2,1)S(1)}, bf16[128,256]{1,0:T(8,128)(2,1)S(1)}, u32[]{:S(2)}, u32[]{:S(2)}) collective-permute-start(bf16[128,256]{1,0:T(8,128)(2,1)S(1)} %get-tuple-element.28), channel_id=1, source_target_pairs={{0,2},{2,0},{4,6},{6,4},{8,10},{10,8},{12,14},{14,12},{1,3},{3,1},... | collective-permute-start | bytes 196616 | tf_op jit(solution)/shard_map/ppermute | solution.py:178
  39.6 1.3 %collective-permute-start.7 = (bf16[128,256]{1,0:T(8,128)(2,1)S(1)}, bf16[128,256]{1,0:T(8,128)(2,1)S(1)}, u32[]{:S(2)}, u32[]{:S(2)}) collective-permute-start(bf16[128,256]{1,0:T(8,128)(2,1)S(1)} %get-tuple-element.30), channel_id=1, source_target_pairs={{0,6},{2,4},{4,2},{6,0},{8,14},{10,12},{12,10},{14,8},{1,7},{3,5},... | collective-permute-start | bytes 196616 | tf_op jit(solution)/shard_map/ppermute | solution.py:178
  40.9 1.6 %collective-permute-start.10 = (bf16[5,128,256]{2,1,0:T(8,128)(2,1)S(1)}, bf16[5,128,256]{2,1,0:T(8,128)(2,1)S(1)}, u32[]{:S(2)}, u32[]{:S(2)}) collective-permute-start(bf16[5,128,256]{2,1,0:T(8,128)(2,1)S(1)} %get-tuple-element.35), channel_id=1, source_target_pairs={{0,12},{4,0},{8,4},{12,8},{1,13},{5,1},{9,5},{13,9},{2,14},{6,2},{... | collective-permute-start | bytes 983048 | tf_op jit(solution)/shard_map/ppermute | solution.py:47
  42.5 2.0 %triplet_body.4.refs_4_.refs_5_ = f32[8,128,256]{2,1,0:T(8,128)S(1)} custom-call(s32[1,1]{1,0:T(1,128)S(6)} %copy.14.refs_0_, s32[1,36]{1,0:T(1,128)S(1)} %copy-done.5, s32[1,36]{1,0:T(1,128)S(1)} %copy-done.6, bf16[36,128,128]{2,1,0:T(8,128)(2,1)S(1)} %bitcast.19, bf16[4,128,256]{2,1,0:T(8,128)(2,1)S(1)} %bitcast.28, bf16[8,128,256]{2,1,0:T(8,128)(2,1)S(1)} %bitcast.29, ...), custom_call_target="tpu_custom_call" | custom-call | flops 575000000 | tf_op jit(solution)/shard_map/triplet_body/pallas_call | solution.py:31
  44.6 1.1 %collective-permute-done.7.refs_3_ = bf16[128,256]{1,0:T(8,128)(2,1)S(1)} collective-permute-done((bf16[128,256]{1,0:T(8,128)(2,1)S(1)}, bf16[128,256]{1,0:T(8,128)(2,1)S(1)}, u32[]{:S(2)}, u32[]{:S(2)}) %collective-permute-start.7) | collective-permute-done | bytes 65568 | tf_op jit(solution)/shard_map/ppermute | solution.py:178
  45.7 1.7 %collective-permute-start.12 = (bf16[128,256]{1,0:T(8,128)(2,1)S(1)}, bf16[128,256]{1,0:T(8,128)(2,1)S(1)}, u32[]{:S(2)}, u32[]{:S(2)}) collective-permute-start(bf16[128,256]{1,0:T(8,128)(2,1)S(1)} %get-tuple-element.39.refs_0_), channel_id=1, source_target_pairs={{0,8},{4,12},{8,0},{12,4},{1,9},{5,13},{9,1},{13,5},{2,10},{6,14},... | collective-permute-start | bytes 196616 | tf_op jit(solution)/shard_map/ppermute | solution.py:182
  47.4 2.1 %collective-permute-start.9 = (bf16[3,128,256]{2,1,0:T(8,128)(2,1)S(1)}, bf16[3,128,256]{2,1,0:T(8,128)(2,1)S(1)}, u32[]{:S(2)}, u32[]{:S(2)}) collective-permute-start(bf16[3,128,256]{2,1,0:T(8,128)(2,1)S(1)} %get-tuple-element.34), channel_id=1, source_target_pairs={{0,12},{4,0},{8,4},{12,8},{1,13},{5,1},{9,5},{13,9},{2,14},{6,2},{... | collective-permute-start | bytes 589832 | tf_op jit(solution)/shard_map/ppermute | solution.py:47
  49.5 1.2 %triplet_body.5.refs_5_.refs_3_ = f32[8,128,256]{2,1,0:T(8,128)S(1)} custom-call(s32[1,1]{1,0:T(1,128)S(6)} %copy.14.refs_0_, s32[1,36]{1,0:T(1,128)S(1)} %copy-done.5, s32[1,36]{1,0:T(1,128)S(1)} %copy-done.6, bf16[36,128,128]{2,1,0:T(8,128)(2,1)S(1)} %bitcast.20, bf16[4,128,256]{2,1,0:T(8,128)(2,1)S(1)} %collective-permute-done.8.refs_0_.refs_4_, ...), custom_call_target="tpu_custom_call" | custom-call | flops 345000000 | tf_op jit(solution)/shard_map/triplet_body/pallas_call | solution.py:31
  50.7 3.3 %collective-permute-done.10.refs_4_.refs_0_ = bf16[5,128,256]{2,1,0:T(8,128)(2,1)S(1)} collective-permute-done((bf16[5,128,256]{2,1,0:T(8,128)(2,1)S(1)}, bf16[5,128,256]{2,1,0:T(8,128)(2,1)S(1)}, u32[]{:S(2)}, u32[]{:S(2)}) %collective-permute-start.10) | collective-permute-done | bytes 327712 | tf_op jit(solution)/shard_map/ppermute | solution.py:47
  54.0 1.2 %triplet_body.6.refs_5_ = f32[8,128,256]{2,1,0:T(8,128)S(1)} custom-call(s32[1,1]{1,0:T(1,128)S(6)} %copy.14.refs_0_, s32[1,36]{1,0:T(1,128)S(1)} %copy-done.5, s32[1,36]{1,0:T(1,128)S(1)} %copy-done.6, bf16[36,128,128]{2,1,0:T(8,128)(2,1)S(1)} %bitcast.21, bf16[5,128,256]{2,1,0:T(8,128)(2,1)S(1)} %collective-permute-done.10.refs_4_.refs_0_, ...), custom_call_target="tpu_custom_call" | custom-call | flops 345000000 | tf_op jit(solution)/shard_map/triplet_body/pallas_call | solution.py:31
  55.3 0.9 %grads_body.1 = (bf16[1024,256]{1,0:T(8,128)(2,1)}, f32[8,128]{1,0:T(8,128)S(1)}) custom-call(f32[1024,256]{1,0:T(8,128)S(1)} %get-tuple-element.36.refs_0_, bf16[1024,256]{1,0:T(8,128)(2,1)S(1)} %collective-permute-done.11.refs_1_), custom_call_target="tpu_custom_call" | custom-call | flops 575000000 | tf_op jit(solution)/shard_map/grads_body/pallas_call | solution.py:31
  56.2 3.0 %collective-permute-start.15 = (bf16[128,256]{1,0:T(8,128)(2,1)S(1)}, bf16[128,256]{1,0:T(8,128)(2,1)S(1)}, u32[]{:S(2)}, u32[]{:S(2)}) collective-permute-start(bf16[128,256]{1,0:T(8,128)(2,1)S(1)} %total_body.3.refs_0_), channel_id=1, source_target_pairs={{0,6},{2,4},{4,2},{6,0},{8,14},{10,12},{12,10},{14,8},{1,7},{3,5},... | collective-permute-start | bytes 196616 | tf_op jit(solution)/shard_map/ppermute | solution.py:178
  59.9 1.8 %triplet_body.7 = bf16[8,128,256]{2,1,0:T(8,128)(2,1)} custom-call(s32[1,1]{1,0:T(1,128)S(6)} %copy.14.refs_0_, s32[1,36]{1,0:T(1,128)S(1)} %copy-done.5, s32[1,36]{1,0:T(1,128)S(1)} %copy-done.6, bf16[36,128,128]{2,1,0:T(8,128)(2,1)S(1)} %bitcast.22, bf16[3,128,256]{2,1,0:T(8,128)(2,1)S(1)} %collective-permute-done.9.refs_4_, ...), custom_call_target="tpu_custom_call" | custom-call | flops 6899999744 | tf_op jit(solution)/shard_map/triplet_body/pallas_call | solution.py:31
  61.7 1.8 %collective-permute-done.14.refs_2_ = bf16[128,256]{1,0:T(8,128)(2,1)S(1)} collective-permute-done((bf16[128,256]{1,0:T(8,128)(2,1)S(1)}, bf16[128,256]{1,0:T(8,128)(2,1)S(1)}, u32[]{:S(2)}, u32[]{:S(2)}) %collective-permute-start.14) | collective-permute-done | bytes 65568 | tf_op jit(solution)/shard_map/ppermute | solution.py:178
  63.5 0.8 %gather_body.1 = f32[512,256]{1,0:T(8,128)} custom-call(bf16[128,256]{1,0:T(8,128)(2,1)S(1)} %total_body.3.refs_0_, bf16[128,256]{1,0:T(8,128)(2,1)S(1)} %collective-permute-done.13.refs_1_, bf16[128,256]{1,0:T(8,128)(2,1)S(1)} %collective-permute-done.14.refs_2_, bf16[128,256]{1,0:T(8,128)(2,1)S(1)} %collective-permute-done.15.refs_3_), custom_call_target="tpu_custom_call" | custom-call | flops 3449999872 | tf_op jit(solution)/shard_map/gather_body/pallas_call | solution.py:31
  (38 shorter events, 3.1 us)
Async XLA Ops:
  0.6 14.5 %collective-permute-start.2 = (bf16[1024,256]{1,0:T(8,128)(2,1)}, bf16[1024,256]{1,0:T(8,128)(2,1)S(1)}, u32[]{:S(2)}, u32[]{:S(2)}) collective-permute-start(bf16[1024,256]{1,0:T(8,128)(2,1)} %bitcast.23), channel_id=1, source_target_pairs={{0,1},{1,0},{2,3},{3,2},{4,5},{5,4},{6,7},{7,6},{8,9},{9,8},{10,11... | collective-permute-start | bytes 1572872 | tf_op jit(solution)/shard_map/ppermute | solution.py:47
  2.1 12.7 %collective-permute-start.3 = (bf16[512,256]{1,0:T(8,128)(2,1)S(1)}, bf16[512,256]{1,0:T(8,128)(2,1)S(1)}, u32[]{:S(2)}, u32[]{:S(2)}) collective-permute-start(bf16[512,256]{1,0:T(8,128)(2,1)S(1)} %slice_bitcast_fusion), channel_id=1, source_target_pairs={{0,4},{4,8},{8,12},{12,0},{1,5},{5,9},{9,13},{13,1},{2,6},{6,10},{... | collective-permute-start | bytes 786440 | tf_op jit(solution)/shard_map/ppermute | solution.py:47
  8.5 6.6 %copy-start.1 = (bf16[1,1024,256]{2,1,0:T(8,128)(2,1)S(1)}, bf16[1,1024,256]{2,1,0:T(8,128)(2,1)}, u32[]{:S(2)}) copy-start(bf16[1,1024,256]{2,1,0:T(8,128)(2,1)} %param.7) | copy-start | bytes 1572868
  8.6 6.6 %copy-start.4 = (bf16[512,256]{1,0:T(8,128)(2,1)S(1)}, bf16[512,256]{1,0:T(8,128)(2,1)}, u32[]{:S(2)}) copy-start(bf16[512,256]{1,0:T(8,128)(2,1)} %refs_5_.1) | copy-start | bytes 786436
  8.6 16.6 %collective-permute-start = (bf16[8,128,256]{2,1,0:T(8,128)(2,1)}, bf16[8,128,256]{2,1,0:T(8,128)(2,1)S(1)}, u32[]{:S(2)}, u32[]{:S(2)}) collective-permute-start(bf16[8,128,256]{2,1,0:T(8,128)(2,1)} %back_body.2.refs_5_), channel_id=1, source_target_pairs={{0,12},{4,0},{8,4},{12,8},{1,13},{5,1},{9,5},{13,9},{2,14},{6,2},{... | collective-permute-start | bytes 1572872 | tf_op jit(solution)/shard_map/ppermute | solution.py:47
  14.8 21.6 %collective-permute-start.1 = (bf16[8,128,256]{2,1,0:T(8,128)(2,1)}, bf16[8,128,256]{2,1,0:T(8,128)(2,1)S(1)}, u32[]{:S(2)}, u32[]{:S(2)}) collective-permute-start(bf16[8,128,256]{2,1,0:T(8,128)(2,1)} %get-tuple-element.23), channel_id=1, source_target_pairs={{0,4},{4,8},{8,12},{12,0},{1,5},{5,9},{9,13},{13,1},{2,6},{6,10},{... | collective-permute-start | bytes 1572872 | tf_op jit(solution)/shard_map/ppermute | solution.py:47
  14.9 1.6 %collective-permute-start.4 = (bf16[512,256]{1,0:T(8,128)(2,1)S(1)}, bf16[512,256]{1,0:T(8,128)(2,1)S(1)}, u32[]{:S(2)}, u32[]{:S(2)}) collective-permute-start(bf16[512,256]{1,0:T(8,128)(2,1)S(1)} %collective-permute-done.3.refs_0_), channel_id=1, source_target_pairs={{0,1},{1,0},{2,3},{3,2},{4,5},{5,4},{6,7},{7,6},{8,9},{9,8},{10,11... | collective-permute-start | bytes 786440 | tf_op jit(solution)/shard_map/ppermute | solution.py:47
  15.9 20.5 %copy-start.2 = (f32[8,128,256]{2,1,0:T(8,128)S(1)}, f32[8,128,256]{2,1,0:T(8,128)}, u32[]{:S(2)}) copy-start(f32[8,128,256]{2,1,0:T(8,128)} %get-tuple-element.22) | copy-start | bytes 3145732
  15.9 20.5 %copy-start.3 = (bf16[1,1024,256]{2,1,0:T(8,128)(2,1)S(1)}, bf16[1,1024,256]{2,1,0:T(8,128)(2,1)}, u32[]{:S(2)}) copy-start(bf16[1,1024,256]{2,1,0:T(8,128)(2,1)} %param.13) | copy-start | bytes 1572868
  15.9 28.6 %collective-permute-start.8 = (bf16[4,128,256]{2,1,0:T(8,128)(2,1)S(1)}, bf16[4,128,256]{2,1,0:T(8,128)(2,1)S(1)}, u32[]{:S(2)}, u32[]{:S(2)}) collective-permute-start(bf16[4,128,256]{2,1,0:T(8,128)(2,1)S(1)} %bitcast.36), channel_id=1, source_target_pairs={{0,4},{4,8},{8,12},{12,0},{1,5},{5,9},{9,13},{13,1},{2,6},{6,10},{... | collective-permute-start | bytes 786440 | tf_op jit(solution)/shard_map/ppermute | solution.py:47
  36.4 6.0 %copy-start = (bf16[1,36,128,128]{3,2,1,0:T(8,128)(2,1)S(1)}, bf16[1,36,128,128]{3,2,1,0:T(8,128)(2,1)}, u32[]{:S(2)}) copy-start(bf16[1,36,128,128]{3,2,1,0:T(8,128)(2,1)} %param.9) | copy-start | bytes 3538948
  36.4 6.0 %copy-start.5 = (s32[1,36]{1,0:T(1,128)S(1)}, s32[1,36]{1,0:T(1,128)}, u32[]{:S(2)}) copy-start(s32[1,36]{1,0:T(1,128)} %refs_1_.11) | copy-start | bytes 436
  36.4 6.0 %copy-start.6 = (s32[1,36]{1,0:T(1,128)S(1)}, s32[1,36]{1,0:T(1,128)}, u32[]{:S(2)}) copy-start(s32[1,36]{1,0:T(1,128)} %refs_2_.15) | copy-start | bytes 436
  37.3 7.3 %collective-permute-start.5 = (bf16[128,256]{1,0:T(8,128)(2,1)S(1)}, bf16[128,256]{1,0:T(8,128)(2,1)S(1)}, u32[]{:S(2)}, u32[]{:S(2)}) collective-permute-start(bf16[128,256]{1,0:T(8,128)(2,1)S(1)} %get-tuple-element.28), channel_id=1, source_target_pairs={{0,2},{2,0},{4,6},{6,4},{8,10},{10,8},{12,14},{14,12},{1,3},{3,1},... | collective-permute-start | bytes 196616 | tf_op jit(solution)/shard_map/ppermute | solution.py:178
  39.2 5.4 %collective-permute-start.6 = (bf16[128,256]{1,0:T(8,128)(2,1)S(1)}, bf16[128,256]{1,0:T(8,128)(2,1)S(1)}, u32[]{:S(2)}, u32[]{:S(2)}) collective-permute-start(bf16[128,256]{1,0:T(8,128)(2,1)S(1)} %get-tuple-element.29), channel_id=1, source_target_pairs={{0,4},{2,6},{4,0},{6,2},{8,12},{10,14},{12,8},{14,10},{1,5},{3,7},... | collective-permute-start | bytes 196616 | tf_op jit(solution)/shard_map/ppermute | solution.py:178
  39.6 6.1 %collective-permute-start.7 = (bf16[128,256]{1,0:T(8,128)(2,1)S(1)}, bf16[128,256]{1,0:T(8,128)(2,1)S(1)}, u32[]{:S(2)}, u32[]{:S(2)}) collective-permute-start(bf16[128,256]{1,0:T(8,128)(2,1)S(1)} %get-tuple-element.30), channel_id=1, source_target_pairs={{0,6},{2,4},{4,2},{6,0},{8,14},{10,12},{12,10},{14,8},{1,7},{3,5},... | collective-permute-start | bytes 196616 | tf_op jit(solution)/shard_map/ppermute | solution.py:178
  40.9 13.1 %collective-permute-start.10 = (bf16[5,128,256]{2,1,0:T(8,128)(2,1)S(1)}, bf16[5,128,256]{2,1,0:T(8,128)(2,1)S(1)}, u32[]{:S(2)}, u32[]{:S(2)}) collective-permute-start(bf16[5,128,256]{2,1,0:T(8,128)(2,1)S(1)} %get-tuple-element.35), channel_id=1, source_target_pairs={{0,12},{4,0},{8,4},{12,8},{1,13},{5,1},{9,5},{13,9},{2,14},{6,2},{... | collective-permute-start | bytes 983048 | tf_op jit(solution)/shard_map/ppermute | solution.py:47
  44.5 10.8 %collective-permute-start.11 = (bf16[1024,256]{1,0:T(8,128)(2,1)S(1)}, bf16[1024,256]{1,0:T(8,128)(2,1)S(1)}, u32[]{:S(2)}, u32[]{:S(2)}) collective-permute-start(bf16[1024,256]{1,0:T(8,128)(2,1)S(1)} %get-tuple-element.37), channel_id=1, source_target_pairs={{0,1},{1,0},{2,3},{3,2},{4,5},{5,4},{6,7},{7,6},{8,9},{9,8},{10,11... | collective-permute-start | bytes 1572872 | tf_op jit(solution)/shard_map/ppermute | solution.py:47
  45.7 10.4 %collective-permute-start.12 = (bf16[128,256]{1,0:T(8,128)(2,1)S(1)}, bf16[128,256]{1,0:T(8,128)(2,1)S(1)}, u32[]{:S(2)}, u32[]{:S(2)}) collective-permute-start(bf16[128,256]{1,0:T(8,128)(2,1)S(1)} %get-tuple-element.39.refs_0_), channel_id=1, source_target_pairs={{0,8},{4,12},{8,0},{12,4},{1,9},{5,13},{9,1},{13,5},{2,10},{6,14},... | collective-permute-start | bytes 196616 | tf_op jit(solution)/shard_map/ppermute | solution.py:182
  47.4 12.5 %collective-permute-start.9 = (bf16[3,128,256]{2,1,0:T(8,128)(2,1)S(1)}, bf16[3,128,256]{2,1,0:T(8,128)(2,1)S(1)}, u32[]{:S(2)}, u32[]{:S(2)}) collective-permute-start(bf16[3,128,256]{2,1,0:T(8,128)(2,1)S(1)} %get-tuple-element.34), channel_id=1, source_target_pairs={{0,12},{4,0},{8,4},{12,8},{1,13},{5,1},{9,5},{13,9},{2,14},{6,2},{... | collective-permute-start | bytes 589832 | tf_op jit(solution)/shard_map/ppermute | solution.py:47
  56.2 5.5 %collective-permute-start.15 = (bf16[128,256]{1,0:T(8,128)(2,1)S(1)}, bf16[128,256]{1,0:T(8,128)(2,1)S(1)}, u32[]{:S(2)}, u32[]{:S(2)}) collective-permute-start(bf16[128,256]{1,0:T(8,128)(2,1)S(1)} %total_body.3.refs_0_), channel_id=1, source_target_pairs={{0,6},{2,4},{4,2},{6,0},{8,14},{10,12},{12,10},{14,8},{1,7},{3,5},... | collective-permute-start | bytes 196616 | tf_op jit(solution)/shard_map/ppermute | solution.py:178
  59.2 4.3 %collective-permute-start.14 = (bf16[128,256]{1,0:T(8,128)(2,1)S(1)}, bf16[128,256]{1,0:T(8,128)(2,1)S(1)}, u32[]{:S(2)}, u32[]{:S(2)}) collective-permute-start(bf16[128,256]{1,0:T(8,128)(2,1)S(1)} %total_body.3.refs_0_), channel_id=1, source_target_pairs={{0,4},{2,6},{4,0},{6,2},{8,12},{10,14},{12,8},{14,10},{1,5},{3,7},... | collective-permute-start | bytes 196616 | tf_op jit(solution)/shard_map/ppermute | solution.py:178
  59.2 4.3 %collective-permute-start.13 = (bf16[128,256]{1,0:T(8,128)(2,1)S(1)}, bf16[128,256]{1,0:T(8,128)(2,1)S(1)}, u32[]{:S(2)}, u32[]{:S(2)}) collective-permute-start(bf16[128,256]{1,0:T(8,128)(2,1)S(1)} %total_body.3.refs_0_), channel_id=1, source_target_pairs={{0,2},{2,0},{4,6},{6,4},{8,10},{10,8},{12,14},{14,12},{1,3},{3,1},... | collective-permute-start | bytes 196616 | tf_op jit(solution)/shard_map/ppermute | solution.py:178
